TPU v7x, 32 devices: a whole 2x2x4 slice. The times are simulated.
32 devices in a mesh: groups: 2 (over x), ctx: 8 (over z, y), width: 2 (over core).
Axes of the slice: x: 2, y: 2, z: 4, core: 2. Of those that a mesh axis runs over, the one named last changes fastest.
Arguments:
- gating_vectors: bfloat16 [2048, 4096], P(('groups', 'ctx'), 'width'), parts along dimension 0, may hold values from -3 to 3
- lookup_vectors: bfloat16 [2048, 4096], P(('groups', 'ctx'), 'width'), parts along dimension 0, may hold values from -3 to 3
- payload_vectors: bfloat16 [2048, 4096], P(('groups', 'ctx'), 'width'), parts along dimension 0, may hold values from -6 to 6
- forgetting_exponent: bfloat16 [2048, 4096], P(('groups', 'ctx'), 'width'), parts along dimension 0, may hold values from 0 to 0.5
- inline_adapt_factor: bfloat16 [2048, 4096], P(('groups', 'ctx'), 'width'), parts along dimension 0, may hold values from 0 to 0.9
- group_layer_scaling: float32 [4096], P('width'), may hold values from 0.5 to 1.5
- group_layer_offset: float32 [4096], P('width'), may hold values from -3 to 3
- present_reward_factor: float32 [4096], P('width'), may hold values from -1 to 1
- shared_dictionary_matrix: bfloat16 [16384, 4096], P('ctx', 'width'), may hold values from -0.09375 to 0.09375
- sparse_code_offset: float32 [16384], P('ctx'), may hold values from -3 to 3
- reconstruct_offset: float32 [4096], P('width'), may hold values from -2 to 2
- panel_holder_choice: int32 [256, 2], P(('groups', 'ctx')), parts along dimension 0, may hold values from 0 to 7, all different within a row; in each aligned block of 16 rows (0 to 15, 16 to 31, ...) at most 8 rows name the same one
- holder_group_enabled: int32 [256, 2, 16], P(('groups', 'ctx')), parts along dimension 0, may hold values 0 or 1
- fixed_feature_slot: int32 [128], P('ctx'), may hold values from 0 to 127
- fixed_feature_amount: float32 [128], P('ctx'), may hold values from 2 to 8
Outputs:
- standardized_mixer_result: bfloat16 [2048, 4096], P(('groups', 'ctx'), 'width'), parts along dimension 0
- steered: bfloat16 [2048, 4096], P(('groups', 'ctx'), 'width'), parts along dimension 0
There are 2 independent parts, one for each index of `groups`. A program takes and returns all parts, laid end to end along the dimension named above; an argument that names none is the same for every part. Nothing has to cross between parts.
Inputs may be any that keep to these rules, and one draw needn't show every extreme that they name: `panel_holder_choice`: each tile names 2 different owners; the tiles of one device name one owner at most 8 times, and in every draw some device's tiles name some owner exactly 8 times.
All inputs are finite; a program needn't handle non-finite values. No bound on the sum of `holder_group_enabled` on one device may be relied on, other than what follows from the above.
Results may differ from a plain program's by a relative error of at most 0.015.
Values may be sent and summed in bfloat16 or wider, within the bound.
A program may use at most 128 MiB of HBM per device.

v0:
```python
import jax
import jax.numpy as jnp
from jax import lax
from jax.sharding import PartitionSpec as P

ATTN_GROUP_DIM = 64
SUB = 32
TILE = 8
BLK = 128
HIGHEST = lax.Precision.HIGHEST


def passed_along(block, axis, distance):
    devices = range(lax.axis_size(axis))
    route = [(i - distance, i) for i in devices if i - distance in devices]
    return lax.ppermute(block, axis, route)


def block_step(carried, pieces):
    rec_in, key_in, val_in, rate_in, learn_in = pieces
    length = rec_in.shape[0]
    removal = key_in * lax.rsqrt(
        jnp.sum(key_in * key_in, -1, keepdims=True) + key_in.shape[-1] * 1e-05
    )
    erase_a = -removal
    erase_b = removal * learn_in
    log_cum = -jnp.cumsum(rate_in, axis=0)
    cum_now = jnp.exp(log_cum)
    cum_prev = jnp.exp(log_cum + rate_in)
    undo = jnp.exp(-log_cum)
    left_a = erase_a * cum_prev
    left_r = rec_in * cum_now
    right_b = erase_b * undo
    right_k = key_in * undo
    row_ids = lax.broadcasted_iota(jnp.int32, (length, length), 0)
    col_ids = lax.broadcasted_iota(jnp.int32, (length, length), 1)
    strict = (row_ids > col_ids).astype(jnp.float32)
    inclusive = (row_ids >= col_ids).astype(jnp.float32)
    mix_ab = jnp.einsum("thk,jhk->htj", left_a, right_b, precision=HIGHEST) * strict
    mix_ak = jnp.einsum("thk,jhk->htj", left_a, right_k, precision=HIGHEST) * strict
    mix_rb = jnp.einsum("thk,jhk->htj", left_r, right_b, precision=HIGHEST) * inclusive
    mix_rk = jnp.einsum("thk,jhk->htj", left_r, right_k, precision=HIGHEST) * inclusive
    padded_v = jnp.concatenate([val_in, jnp.zeros_like(val_in)], -1)
    target = jnp.einsum("thk,hxk->htx", left_a, carried, precision=HIGHEST) + jnp.einsum(
        "htj,jhx->htx", mix_ak, padded_v, precision=HIGHEST
    )
    inverse = jnp.eye(length, dtype=jnp.float32)[None] + mix_ab
    power = mix_ab
    for doubling in range(length.bit_length() - 2):
        power = jnp.einsum("hij,hjk->hik", power, power, precision=HIGHEST)
        inverse = inverse + jnp.einsum("hij,hjk->hik", inverse, power, precision=HIGHEST)
    reads = jnp.einsum("htj,hjx->htx", inverse, target, precision=HIGHEST)
    outputs = (
        jnp.einsum("thk,hxk->htx", left_r, carried, precision=HIGHEST)
        + jnp.einsum("htj,hjx->htx", mix_rb, reads, precision=HIGHEST)
        + jnp.einsum("htj,jhx->htx", mix_rk, padded_v, precision=HIGHEST)
    )
    fade = cum_now[-1]
    updated = (
        carried
        + jnp.einsum("hjx,jhk->hxk", reads, right_b, precision=HIGHEST)
        + jnp.einsum("jhx,jhk->hxk", padded_v, right_k, precision=HIGHEST)
    )
    return (updated * fade[:, None, :], outputs)


def activate(preacts, mask_vals, index_vals, value_vals):
    senders, items, block_count = mask_vals.shape
    codes = jnp.maximum(preacts, 0.0).reshape(senders, items, TILE, block_count, BLK)
    within = lax.broadcasted_iota(jnp.int32, (block_count, BLK), 1)
    hit = within == index_vals[:, None]
    codes = jnp.where(hit, value_vals[:, None], codes)
    codes = codes * mask_vals.astype(jnp.float32)[:, :, None, :, None]
    return codes.reshape(senders * items * TILE, block_count * BLK).astype(jnp.bfloat16)


def body(
    gating_vectors,
    lookup_vectors,
    payload_vectors,
    forgetting_exponent,
    inline_adapt_factor,
    group_layer_scaling,
    group_layer_offset,
    present_reward_factor,
    shared_dictionary_matrix,
    sparse_code_offset,
    reconstruct_offset,
    panel_holder_choice,
    holder_group_enabled,
    fixed_feature_slot,
    fixed_feature_amount,
):
    tok_rows = gating_vectors.shape[0]
    feat_local = gating_vectors.shape[1]
    group_counting = feat_local // ATTN_GROUP_DIM
    gating_vectors_all = gating_vectors.astype(jnp.float32).reshape(
        tok_rows, group_counting, ATTN_GROUP_DIM
    )
    lookup_vectors_all = lookup_vectors.astype(jnp.float32).reshape(
        tok_rows, group_counting, ATTN_GROUP_DIM
    )
    payload_vectors_all = payload_vectors.astype(jnp.float32).reshape(
        tok_rows, group_counting, ATTN_GROUP_DIM
    )
    rate_all = forgetting_exponent.astype(jnp.float32).reshape(
        tok_rows, group_counting, ATTN_GROUP_DIM
    )
    learn_all = inline_adapt_factor.astype(jnp.float32).reshape(
        tok_rows, group_counting, ATTN_GROUP_DIM
    )
    block_count = tok_rows // SUB

    def stacked(array):
        return array.reshape(block_count, SUB, group_counting, ATTN_GROUP_DIM)

    eye_heads = jnp.broadcast_to(
        jnp.eye(ATTN_GROUP_DIM, dtype=jnp.float32), (group_counting, ATTN_GROUP_DIM, ATTN_GROUP_DIM)
    )
    zero_heads = jnp.zeros((group_counting, ATTN_GROUP_DIM, ATTN_GROUP_DIM), jnp.float32)
    start_state = jnp.concatenate([zero_heads, eye_heads], axis=1)
    final_state, block_outs = lax.scan(
        block_step,
        start_state,
        (
            stacked(gating_vectors_all),
            stacked(lookup_vectors_all),
            stacked(payload_vectors_all),
            stacked(rate_all),
            stacked(learn_all),
        ),
    )
    block_outs = block_outs.transpose(0, 2, 1, 3).reshape(
        tok_rows, group_counting, 2 * ATTN_GROUP_DIM
    )
    local_out = block_outs[:, :, :ATTN_GROUP_DIM]
    probe = block_outs[:, :, ATTN_GROUP_DIM:]
    own_state = final_state[:, :ATTN_GROUP_DIM, :]
    transfer = final_state[:, ATTN_GROUP_DIM:, :]

    def forward(counter, carry_pair):
        incoming = passed_along(carry_pair[1], "ctx", 1)
        leaving = jnp.einsum("hvj,hjk->hvk", incoming, transfer, precision=HIGHEST) + own_state
        return (incoming, leaving)

    prior = lax.fori_loop(0, lax.axis_size("ctx") - 1, forward, (zero_heads, own_state))[0]
    wkv = local_out + jnp.einsum("hvk,thk->thv", prior, probe, precision=HIGHEST)
    center = wkv - jnp.mean(wkv, -1, keepdims=True)
    spread = jnp.mean(center * center, -1, keepdims=True)
    standardized_lines = (center * lax.rsqrt(spread + 1e-05)).reshape(
        tok_rows, feat_local
    ) * group_layer_scaling + group_layer_offset
    present_reward = (
        jnp.sum(
            gating_vectors_all
            * lookup_vectors_all
            * present_reward_factor.reshape(group_counting, ATTN_GROUP_DIM),
            -1,
            keepdims=True,
        )
        * payload_vectors_all
    ).reshape(tok_rows, feat_local)
    standardized_mixer_result = (standardized_lines + present_reward).astype(jnp.bfloat16)
    enc_in = (standardized_mixer_result.astype(jnp.float32) - reconstruct_offset).astype(
        jnp.bfloat16
    )
    ctx_count = lax.axis_size("ctx")
    tile_count = tok_rows // TILE
    slot_count = panel_holder_choice.shape[1]
    blocks_own = holder_group_enabled.shape[2]
    capacity = max(2, 2 * tok_rows * slot_count // (TILE * ctx_count))
    pair_count = tile_count * slot_count
    owner_flat = panel_holder_choice.reshape(pair_count)
    owner_hot = (owner_flat[:, None] == lax.broadcasted_iota(jnp.int32, (1, ctx_count), 1)).astype(
        jnp.int32
    )
    ranks = jnp.sum((jnp.cumsum(owner_hot, axis=0) - owner_hot) * owner_hot, axis=1)
    slot_ids = owner_flat * capacity + ranks
    dispatch = (
        slot_ids[None, :] == lax.broadcasted_iota(jnp.int32, (ctx_count * capacity, 1), 0)
    ).astype(jnp.float32)
    tile_pick = (
        lax.broadcasted_iota(jnp.int32, (tile_count, pair_count), 1) // slot_count
        == lax.broadcasted_iota(jnp.int32, (tile_count, pair_count), 0)
    ).astype(jnp.float32)
    slot_tile = jnp.dot(dispatch, tile_pick.T)
    send_rows = jnp.dot(
        slot_tile.astype(jnp.bfloat16),
        enc_in.reshape(tile_count, TILE * feat_local),
        preferred_element_type=jnp.float32,
    )
    send_rows = send_rows.astype(jnp.bfloat16).reshape(ctx_count, capacity, TILE, feat_local)
    send_mask = jnp.dot(
        dispatch, holder_group_enabled.reshape(pair_count, blocks_own).astype(jnp.float32)
    )
    send_mask = send_mask.astype(jnp.bfloat16).reshape(ctx_count, capacity, blocks_own)
    got_rows = lax.all_to_all(send_rows, "ctx", split_axis=0, concat_axis=0, tiled=True)
    got_mask = lax.all_to_all(send_mask, "ctx", split_axis=0, concat_axis=0, tiled=True)
    senders = got_rows.shape[0]
    items = got_rows.shape[1]
    flat_rows = got_rows.reshape(senders * items * TILE, feat_local)
    partial_pre = lax.dot_general(
        flat_rows,
        shared_dictionary_matrix,
        (((1,), (1,)), ((), ())),
        preferred_element_type=jnp.float32,
    )
    total_pre = lax.psum(partial_pre.astype(jnp.bfloat16), "width").astype(jnp.float32)
    codes = activate(
        total_pre + sparse_code_offset, got_mask, fixed_feature_slot, fixed_feature_amount
    )
    decoded = jnp.dot(codes, shared_dictionary_matrix, preferred_element_type=jnp.float32).astype(
        jnp.bfloat16
    )
    returned = decoded.reshape(senders, items, TILE, feat_local)
    received = lax.all_to_all(returned, "ctx", split_axis=0, concat_axis=0, tiled=True)
    summed = jnp.dot(
        slot_tile.T.astype(jnp.bfloat16),
        received.reshape(ctx_count * capacity, TILE * feat_local),
        preferred_element_type=jnp.float32,
    )
    steered = (summed.reshape(tok_rows, feat_local) + reconstruct_offset).astype(jnp.bfloat16)
    return (standardized_mixer_result, steered)


def solution(mesh):
    placed = (
        P(("groups", "ctx"), "width"),
        P(("groups", "ctx"), "width"),
        P(("groups", "ctx"), "width"),
        P(("groups", "ctx"), "width"),
        P(("groups", "ctx"), "width"),
        P("width"),
        P("width"),
        P("width"),
        P("ctx", "width"),
        P("ctx"),
        P("width"),
        P(("groups", "ctx"), None),
        P(("groups", "ctx"), None, None),
        P("ctx"),
        P("ctx"),
    )
    return jax.shard_map(
        body,
        mesh=mesh,
        in_specs=placed,
        out_specs=(P(("groups", "ctx"), "width"), P(("groups", "ctx"), "width")),
        check_vma=False,
    )
```

profile of v0, /device:TPU:0, one launch (start us, length us, event | category | flops | bytes accessed | tf_op | source)
XLA Modules:
  0.0 519.1 jit_solution(18060309378639857099)
XLA Ops:
  26.0 119.1 %while.24 = (s32[]{:T(128)}, f32[32,128,64]{1,2,0:T(8,128)S(1)}, f32[4,32,32,128]{3,1,2,0:T(8,128)}, f32[4,32,32,64]{3,2,1,0:T(8,128)S(1)}, f32[4,32,32,64]{3,2,...) while((s32[]{:T(128)}, f32[32,128,64]{1,2,0:T(8,128)S(1)}, ...), condition=%wide.region_3.4_spmd, body=%wide.region_0.3_spmd.sunk | while | flops 809539584 | bytes 26289764 | solution.py:122
  149.7 4.8 fusion.64
  158.2 189.7 %while.25 = (s32[]{:T(128)}, f32[32,64,64]{2,1,0:T(8,128)}, f32[32,64,64]{2,1,0:T(8,128)}, f32[32,64,64]{2,1,0:T(8,128)S(1)}, f32[32,64,64]{2,1,0:T(8,128)S(1)}, /*index=5*/s32[]{:T(128)}) while((s32[]{:T(128)}, f32[32,64,64]{2,1,0:T(8,128)}, f32[32,64,64]{2,1,0:T(8,128)}, f32[32,64,64]{2,1,0:T(8,128)S(1)}, f32[32,64,64]{2,1,0:T(8,128)S(1)}, ...), condition=%wide.region_5.6_spmd, body=%wide.region_4.5_spmd.sunk | while | flops 100794368 | bytes 6291593 | solution.py:146
  158.2 4.9 collective-permute-start
  163.1 22.7 %collective-permute-done = f32[32,64,64]{2,1,0:T(8,128)S(1)} collective-permute-done((f32[32,64,64]{2,1,0:T(8,128)}, f32[32,64,64]{2,1,0:T(8,128)S(1)}, u32[]{:S(2)}, u32[]{:S(2)}) %collective-permute-start) | collective-permute-done | bytes 524320 | tf_op jit(solution)/shard_map/while/body/eval_jaxpr/ppermute | solution.py:16
  192.4 21.8 %collective-permute-done = f32[32,64,64]{2,1,0:T(8,128)S(1)} collective-permute-done((f32[32,64,64]{2,1,0:T(8,128)}, f32[32,64,64]{2,1,0:T(8,128)S(1)}, u32[]{:S(2)}, u32[]{:S(2)}) %collective-permute-start) | collective-permute-done | bytes 524320 | tf_op jit(solution)/shard_map/while/body/eval_jaxpr/ppermute | solution.py:16
  216.4 4.4 collective-permute-start
  220.7 20.9 %collective-permute-done = f32[32,64,64]{2,1,0:T(8,128)S(1)} collective-permute-done((f32[32,64,64]{2,1,0:T(8,128)}, f32[32,64,64]{2,1,0:T(8,128)S(1)}, u32[]{:S(2)}, u32[]{:S(2)}) %collective-permute-start) | collective-permute-done | bytes 524320 | tf_op jit(solution)/shard_map/while/body/eval_jaxpr/ppermute | solution.py:16
  243.8 5.2 %collective-permute-start = (f32[32,64,64]{2,1,0:T(8,128)}, f32[32,64,64]{2,1,0:T(8,128)S(1)}, u32[]{:S(2)}, u32[]{:S(2)}) collective-permute-start(f32[32,64,64]{2,1,0:T(8,128)} %get-tuple-element.269), channel_id=1, source_target_pairs={{0,2},{2,4},{4,6},{6,8},{8,10},{10,12},{12,14},{1,3},{3,5},{5,7},{... | collective-permute-start | bytes 1572872 | tf_op jit(solution)/shard_map/while/body/eval_jaxpr/ppermute | solution.py:16
  249.1 19.9 %collective-permute-done = f32[32,64,64]{2,1,0:T(8,128)S(1)} collective-permute-done((f32[32,64,64]{2,1,0:T(8,128)}, f32[32,64,64]{2,1,0:T(8,128)S(1)}, u32[]{:S(2)}, u32[]{:S(2)}) %collective-permute-start) | collective-permute-done | bytes 524320 | tf_op jit(solution)/shard_map/while/body/eval_jaxpr/ppermute | solution.py:16
  271.2 5.2 %collective-permute-start = (f32[32,64,64]{2,1,0:T(8,128)}, f32[32,64,64]{2,1,0:T(8,128)S(1)}, u32[]{:S(2)}, u32[]{:S(2)}) collective-permute-start(f32[32,64,64]{2,1,0:T(8,128)} %get-tuple-element.269), channel_id=1, source_target_pairs={{0,2},{2,4},{4,6},{6,8},{8,10},{10,12},{12,14},{1,3},{3,5},{5,7},{... | collective-permute-start | bytes 1572872 | tf_op jit(solution)/shard_map/while/body/eval_jaxpr/ppermute | solution.py:16
  276.5 19.0 %collective-permute-done = f32[32,64,64]{2,1,0:T(8,128)S(1)} collective-permute-done((f32[32,64,64]{2,1,0:T(8,128)}, f32[32,64,64]{2,1,0:T(8,128)S(1)}, u32[]{:S(2)}, u32[]{:S(2)}) %collective-permute-start) | collective-permute-done | bytes 524320 | tf_op jit(solution)/shard_map/while/body/eval_jaxpr/ppermute | solution.py:16
  297.7 5.2 %collective-permute-start = (f32[32,64,64]{2,1,0:T(8,128)}, f32[32,64,64]{2,1,0:T(8,128)S(1)}, u32[]{:S(2)}, u32[]{:S(2)}) collective-permute-start(f32[32,64,64]{2,1,0:T(8,128)} %get-tuple-element.269), channel_id=1, source_target_pairs={{0,2},{2,4},{4,6},{6,8},{8,10},{10,12},{12,14},{1,3},{3,5},{5,7},{... | collective-permute-start | bytes 1572872 | tf_op jit(solution)/shard_map/while/body/eval_jaxpr/ppermute | solution.py:16
  303.0 18.1 %collective-permute-done = f32[32,64,64]{2,1,0:T(8,128)S(1)} collective-permute-done((f32[32,64,64]{2,1,0:T(8,128)}, f32[32,64,64]{2,1,0:T(8,128)S(1)}, u32[]{:S(2)}, u32[]{:S(2)}) %collective-permute-start) | collective-permute-done | bytes 524320 | tf_op jit(solution)/shard_map/while/body/eval_jaxpr/ppermute | solution.py:16
  323.3 5.2 %collective-permute-start = (f32[32,64,64]{2,1,0:T(8,128)}, f32[32,64,64]{2,1,0:T(8,128)S(1)}, u32[]{:S(2)}, u32[]{:S(2)}) collective-permute-start(f32[32,64,64]{2,1,0:T(8,128)} %get-tuple-element.269), channel_id=1, source_target_pairs={{0,2},{2,4},{4,6},{6,8},{8,10},{10,12},{12,14},{1,3},{3,5},{5,7},{... | collective-permute-start | bytes 1572872 | tf_op jit(solution)/shard_map/while/body/eval_jaxpr/ppermute | solution.py:16
  328.5 17.2 %collective-permute-done = f32[32,64,64]{2,1,0:T(8,128)S(1)} collective-permute-done((f32[32,64,64]{2,1,0:T(8,128)}, f32[32,64,64]{2,1,0:T(8,128)S(1)}, u32[]{:S(2)}, u32[]{:S(2)}) %collective-permute-start) | collective-permute-done | bytes 524320 | tf_op jit(solution)/shard_map/while/body/eval_jaxpr/ppermute | solution.py:16
  347.9 7.0 %fusion.66 = (f32[128,32]{0,1:T(8,128)S(1)}, f32[128,32,64]{0,2,1:T(8,128)S(1)}) fusion(f32[128,32,64]{0,2,1:T(8,128)} %copy.85, f32[32,64,64]{2,1,0:T(8,128)} %get-tuple-element.73, f32[128,32,64]{2,1,0:T(8,128)} %get-tuple-element.138), kind=kOutput, calls=%fused_computation.118 | convolution fusion | flops 201846784 | bytes 3686400 | tf_op jit(solution)/shard_map/hvk,thk->thv/dot_general | solution.py:147
  363.4 50.3 %all_to_all.15 = bf16[8,8,8,2048]{3,2,1,0:T(8,128)(2,1)S(1)} all-to-all(bf16[8,8,8,2048]{3,2,1,0:T(8,128)(2,1)S(1)} %copy.77), channel_id=1, replica_groups=mesh['groups'=2,'ctx'=8,'width'=2] {'ctx'}, dimensions={0} | all-to-all | bytes 4194304 | tf_op jit(solution)/shard_map/all_to_all | solution.py:197
  413.7 9.1 %convolution_convert_fusion.2 = bf16[512,2048]{1,0:T(8,128)(2,1)} fusion(bf16[512,2048]{1,0:T(8,128)(2,1)S(1)} %bitcast.176, bf16[2048,2048]{1,0:T(8,128)(2,1)} %param.27), kind=kOutput, calls=%fused_computation.68 | convolution fusion | flops 4296015872 | bytes 12582912 | tf_op jit(solution)/shard_map/dot_general | solution.py:202
  428.2 6.4 %all-to-all-done.1 = bf16[8,8,16]{2,1,0:T(8,128)(2,1)S(1)} async-done(((bf16[8,8,16]{2,1,0:T(8,128)(2,1)}), bf16[8,8,16]{2,1,0:T(8,128)(2,1)S(1)}, u32[]{:S(2)}, u32[]{:S(2)}) %all-to-all-start.1) | async-done | bytes 2080 | tf_op jit(solution)/shard_map/all_to_all | solution.py:198
  434.6 8.6 %all-reduce.4.cloned.1.call-done = bf16[512,2048]{1,0:T(8,128)(2,1)} async-done(((bf16[512,2048]{1,0:T(8,128)(2,1)}), bf16[512,2048]{1,0:T(8,128)(2,1)}) %all-reduce.4.cloned.1.call-update) | async-done | bytes 2097168 | tf_op jit(solution)/shard_map/psum | solution.py:208
  444.9 9.2 %convolution_convert_fusion.1 = bf16[512,2048]{1,0:T(8,128)(2,1)} fusion(bf16[2048,2048]{1,0:T(8,128)(2,1)} %param.27, f32[512,2048]{1,0:T(8,128)S(1)} %bitcast.173, bf16[512,2048]{1,0:T(8,128)(2,1)S(1)} %copy-done.15, f32[2048]{0:T(1024)S(1)} %copy-done.16, f32[2048]{0:T(1024)S(1)} %broadcast_bitcast_fusion, pred[2048]{0:T(1024)(128)(4,1)S(1)} %fusion.58), kind=kOutput, calls=%fused_computation.67 | convolution fusion | flops 4302307328 | bytes 16795648 | tf_op jit(solution)/shard_map/dot_general | solution.py:212
  454.1 5.8 %all-to-all-start.2 = ((bf16[8,8,8,2048]{3,2,1,0:T(8,128)(2,1)}), bf16[8,8,8,2048]{3,2,1,0:T(8,128)(2,1)S(1)}, u32[]{:S(2)}, u32[]{:S(2)}) async-start(bf16[8,8,8,2048]{3,2,1,0:T(8,128)(2,1)} %bitcast.175), calls=%async_computation.2 | async-start | bytes 4194304 | tf_op jit(solution)/shard_map/all_to_all | solution.py:216
  460.9 47.7 %all-to-all-done.2 = bf16[8,8,8,2048]{3,2,1,0:T(8,128)(2,1)S(1)} async-done(((bf16[8,8,8,2048]{3,2,1,0:T(8,128)(2,1)}), bf16[8,8,8,2048]{3,2,1,0:T(8,128)(2,1)S(1)}, u32[]{:S(2)}, u32[]{:S(2)}) %all-to-all-start.2) | async-done | bytes 2097184 | tf_op jit(solution)/shard_map/all_to_all | solution.py:216
  (231 shorter events, 169.7 us)
Async XLA Ops:
  7.2 420.9 %copy-start = (f32[16]{0:T(128)S(1)}, f32[16]{0:T(128)}, u32[]{:S(2)}) copy-start(f32[16]{0:T(128)} %param.33) | copy-start | bytes 196
  7.2 436.1 %all-reduce.4.cloned.1.call-start = ((), (), s32[]{:S(2)}) async-start(), calls=%async_computation.3 | async-start | bytes 4194304 | tf_op jit(solution)/shard_map/psum | solution.py:208
  13.6 4.3 copy-start.2
  17.9 3.1 copy-start.5
  21.0 2.3 copy-start.6
  158.2 27.6 %collective-permute-start = (f32[32,64,64]{2,1,0:T(8,128)}, f32[32,64,64]{2,1,0:T(8,128)S(1)}, u32[]{:S(2)}, u32[]{:S(2)}) collective-permute-start(f32[32,64,64]{2,1,0:T(8,128)} %get-tuple-element.269), channel_id=1, source_target_pairs={{0,2},{2,4},{4,6},{6,8},{8,10},{10,12},{12,14},{1,3},{3,5},{5,7},{... | collective-permute-start | bytes 1572872 | tf_op jit(solution)/shard_map/while/body/eval_jaxpr/ppermute | solution.py:16
  185.8 2.2 copy-start.1
  188.0 26.1 %collective-permute-start = (f32[32,64,64]{2,1,0:T(8,128)}, f32[32,64,64]{2,1,0:T(8,128)S(1)}, u32[]{:S(2)}, u32[]{:S(2)}) collective-permute-start(f32[32,64,64]{2,1,0:T(8,128)} %get-tuple-element.269), channel_id=1, source_target_pairs={{0,2},{2,4},{4,6},{6,8},{8,10},{10,12},{12,14},{1,3},{3,5},{5,7},{... | collective-permute-start | bytes 1572872 | tf_op jit(solution)/shard_map/while/body/eval_jaxpr/ppermute | solution.py:16
  216.4 25.2 %collective-permute-start = (f32[32,64,64]{2,1,0:T(8,128)}, f32[32,64,64]{2,1,0:T(8,128)S(1)}, u32[]{:S(2)}, u32[]{:S(2)}) collective-permute-start(f32[32,64,64]{2,1,0:T(8,128)} %get-tuple-element.269), channel_id=1, source_target_pairs={{0,2},{2,4},{4,6},{6,8},{8,10},{10,12},{12,14},{1,3},{3,5},{5,7},{... | collective-permute-start | bytes 1572872 | tf_op jit(solution)/shard_map/while/body/eval_jaxpr/ppermute | solution.py:16
  241.6 2.2 copy-start.1
  243.8 25.2 %collective-permute-start = (f32[32,64,64]{2,1,0:T(8,128)}, f32[32,64,64]{2,1,0:T(8,128)S(1)}, u32[]{:S(2)}, u32[]{:S(2)}) collective-permute-start(f32[32,64,64]{2,1,0:T(8,128)} %get-tuple-element.269), channel_id=1, source_target_pairs={{0,2},{2,4},{4,6},{6,8},{8,10},{10,12},{12,14},{1,3},{3,5},{5,7},{... | collective-permute-start | bytes 1572872 | tf_op jit(solution)/shard_map/while/body/eval_jaxpr/ppermute | solution.py:16
  269.0 2.2 copy-start.1
  271.2 24.2 %collective-permute-start = (f32[32,64,64]{2,1,0:T(8,128)}, f32[32,64,64]{2,1,0:T(8,128)S(1)}, u32[]{:S(2)}, u32[]{:S(2)}) collective-permute-start(f32[32,64,64]{2,1,0:T(8,128)} %get-tuple-element.269), channel_id=1, source_target_pairs={{0,2},{2,4},{4,6},{6,8},{8,10},{10,12},{12,14},{1,3},{3,5},{5,7},{... | collective-permute-start | bytes 1572872 | tf_op jit(solution)/shard_map/while/body/eval_jaxpr/ppermute | solution.py:16
  297.7 23.3 %collective-permute-start = (f32[32,64,64]{2,1,0:T(8,128)}, f32[32,64,64]{2,1,0:T(8,128)S(1)}, u32[]{:S(2)}, u32[]{:S(2)}) collective-permute-start(f32[32,64,64]{2,1,0:T(8,128)} %get-tuple-element.269), channel_id=1, source_target_pairs={{0,2},{2,4},{4,6},{6,8},{8,10},{10,12},{12,14},{1,3},{3,5},{5,7},{... | collective-permute-start | bytes 1572872 | tf_op jit(solution)/shard_map/while/body/eval_jaxpr/ppermute | solution.py:16
  323.3 22.4 %collective-permute-start = (f32[32,64,64]{2,1,0:T(8,128)}, f32[32,64,64]{2,1,0:T(8,128)S(1)}, u32[]{:S(2)}, u32[]{:S(2)}) collective-permute-start(f32[32,64,64]{2,1,0:T(8,128)} %get-tuple-element.269), channel_id=1, source_target_pairs={{0,2},{2,4},{4,6},{6,8},{8,10},{10,12},{12,14},{1,3},{3,5},{5,7},{... | collective-permute-start | bytes 1572872 | tf_op jit(solution)/shard_map/while/body/eval_jaxpr/ppermute | solution.py:16
  345.7 2.2 copy-start.1
  355.1 3.9 copy-start.3
  355.1 3.9 copy-start.8
  355.1 3.9 copy-start.10
  355.1 3.9 copy-start.11
  422.8 5.3 %copy-start.14 = (s32[16]{0:T(128)S(1)}, s32[16]{0:T(128)}, u32[]{:S(2)}) copy-start(s32[16]{0:T(128)} %param.32) | copy-start | bytes 196
  424.4 10.2 %all-to-all-start.1 = ((bf16[8,8,16]{2,1,0:T(8,128)(2,1)}), bf16[8,8,16]{2,1,0:T(8,128)(2,1)S(1)}, u32[]{:S(2)}, u32[]{:S(2)}) async-start(bf16[8,8,16]{2,1,0:T(8,128)(2,1)} %bitcast.19), calls=%async_computation.1 | async-start | bytes 32768 | tf_op jit(solution)/shard_map/all_to_all | solution.py:198
  428.2 16.2 %copy-start.16 = (f32[2048]{0:T(1024)S(1)}, f32[2048]{0:T(1024)}, u32[]{:S(2)}) copy-start(f32[2048]{0:T(1024)} %param.28) | copy-start | bytes 24580
  454.1 54.5 %all-to-all-start.2 = ((bf16[8,8,8,2048]{3,2,1,0:T(8,128)(2,1)}), bf16[8,8,8,2048]{3,2,1,0:T(8,128)(2,1)S(1)}, u32[]{:S(2)}, u32[]{:S(2)}) async-start(bf16[8,8,8,2048]{3,2,1,0:T(8,128)(2,1)} %bitcast.175), calls=%async_computation.2 | async-start | bytes 4194304 | tf_op jit(solution)/shard_map/all_to_all | solution.py:216
  (9 other events, 14.3 us)
Sparse Core Ops, SparseCore 0:
  423.0 20.2 all-reduce.3
where the time goes:
time: 525 us; the launch traced here: 519 us
  waiting for transfers between devices  202 us (38%)
  matrix products  127 us (24%)
  local copies, waits for them, and re-layouts  50.3 us (10%)
  blocking collectives  50.3 us (10%)
  starting transfers between devices  44 us (8%)
  loops' own time  16.2 us (3%)
  other arithmetic  15 us (3%)
  between operations  14.6 us (3%)
    ppermute x7, waiting for transfers between devices, passed_along(): return lax.ppermute(block, axis, route)  139 us
    all_to_all x1, blocking collectives, body(): lax.all_to_all(send_rows, 'ctx', split_axis=0, concat_axis=0, tiled=True)  50.3 us
    all_to_all x1, waiting for transfers between devices, body(): lax.all_to_all(returned, 'ctx', split_axis=0, concat_axis=0, tiled=True)  47.7 us
    ppermute x7, starting transfers between devices, passed_along(): return lax.ppermute(block, axis, route)  34.6 us
    another operation x1, loops' own time, body(): lax.scan(block_step, start_state, (stacked(gating_vectors_all), stacked(l...  16.1 us
    dot_general x7, matrix products, forward(): jnp.einsum('hvj,hjk->hvk', incoming, transfer, precision=HIGHEST)  15.6 us
    unnamed x41, local copies, waits for them, and re-layouts  12.8 us
    another operation x5, local copies, waits for them, and re-layouts, stacked(): return array.reshape(block_count, SUB, group_counting, ATTN_GROUP_DIM)  11.5 us
  transfers between devices with their start and end apart: 10, of which 10 were waited for; matrix products, arithmetic and copies ran while one was open for 0% of the time, Pallas kernels for 0%

commit v1 on v0

--- a/solution.py
+++ b/solution.py
@@ -1,13 +1,34 @@
+import functools
 import jax
 import jax.numpy as jnp
 from jax import lax
 from jax.sharding import PartitionSpec as P
+from jax.lax import axis_index, ppermute, psum
 
 ATTN_GROUP_DIM = 64
 SUB = 32
 TILE = 8
 BLK = 128
 HIGHEST = lax.Precision.HIGHEST
+
+
+def fill_the_columns(local, a_name):
+    outcome_arr, y = (psum(1, a_name), axis_index(a_name))
+    reached = local.shape[0] // outcome_arr
+    arr_out = list(local.shape)
+    arr_out[0] = reached
+    part_next = arr_out[0]
+    arr_out[0] = part_next * outcome_arr
+    mixed_arr = jnp.zeros(arr_out, local.dtype)
+    for s in range(outcome_arr):
+        y_new = lax.dynamic_slice_in_dim(local, (y ^ s) * reached, reached, axis=0)
+        if s:
+            y_new = ppermute(y_new, a_name, [(dev_j, dev_j ^ s) for dev_j in range(outcome_arr)])
+        mixed_arr = lax.dynamic_update_slice_in_dim(mixed_arr, y_new, (y ^ s) * part_next, axis=0)
+    return mixed_arr
+
+
+tasks_shape = functools.partial(fill_the_columns, a_name="ctx")
 
 
 def passed_along(block, axis, distance):
@@ -194,7 +215,7 @@
         dispatch, holder_group_enabled.reshape(pair_count, blocks_own).astype(jnp.float32)
     )
     send_mask = send_mask.astype(jnp.bfloat16).reshape(ctx_count, capacity, blocks_own)
-    got_rows = lax.all_to_all(send_rows, "ctx", split_axis=0, concat_axis=0, tiled=True)
+    got_rows = tasks_shape(send_rows)
     got_mask = lax.all_to_all(send_mask, "ctx", split_axis=0, concat_axis=0, tiled=True)
     senders = got_rows.shape[0]
     items = got_rows.shape[1]

time: 525 us -> 524 us (level)
  blocking collectives: 50.3 us -> 0 us
  starting transfers between devices: 44 us -> 71.1 us
  waiting for transfers between devices: 202 us -> 224 us
    all_to_all x1 -> x0, blocking collectives: 50.3 us -> none  [body(): lax.all_to_all(send_rows, 'ctx', split_axis=0, concat_axis=0, tiled=True)]
    ppermute x0 -> x7, waiting for transfers between devices: none -> 21.5 us  [fill_the_columns(): ppermute(y_new, a_name, [(dev_j, dev_j ^ s) for dev_j in range(outcome_ar...]
    ppermute x0 -> x7, starting transfers between devices: none -> 20 us  [fill_the_columns(): ppermute(y_new, a_name, [(dev_j, dev_j ^ s) for dev_j in range(outcome_ar...]
    all_to_all x1, starting transfers between devices: 3.6 us -> 10.8 us  [body(): lax.all_to_all(send_mask, 'ctx', split_axis=0, concat_axis=0, tiled=True)]
    unnamed x41 -> x48, local copies, waits for them, and re-layouts: 12.8 us -> 13.9 us
  transfers between devices with their start and end apart: 10 -> 17, of which waited for: 10 -> 13; matrix products, arithmetic and copies ran while one was open for 0% -> 1% of each run, Pallas kernels for 0% -> 0%
where the time goes in v1:
time: 524 us; the launch traced here: 519 us
  waiting for transfers between devices  224 us (43%)
  matrix products  127 us (24%)
  starting transfers between devices  71.1 us (14%)
  local copies, waits for them, and re-layouts  51 us (10%)
  loops' own time  16.2 us (3%)
  other arithmetic  15.2 us (3%)
  between operations  14.8 us (3%)
    ppermute x7, waiting for transfers between devices, passed_along(): return lax.ppermute(block, axis, route)  139 us
    all_to_all x1, waiting for transfers between devices, body(): lax.all_to_all(returned, 'ctx', split_axis=0, concat_axis=0, tiled=True)  47.7 us
    ppermute x7, starting transfers between devices, passed_along(): return lax.ppermute(block, axis, route)  34.6 us
    ppermute x7, waiting for transfers between devices, fill_the_columns(): ppermute(y_new, a_name, [(dev_j, dev_j ^ s) for dev_j in range(outcome_ar...  21.5 us
    ppermute x7, starting transfers between devices, fill_the_columns(): ppermute(y_new, a_name, [(dev_j, dev_j ^ s) for dev_j in range(outcome_ar...  20 us
    another operation x1, loops' own time, body(): lax.scan(block_step, start_state, (stacked(gating_vectors_all), stacked(l...  16.1 us
    dot_general x7, matrix products, forward(): jnp.einsum('hvj,hjk->hvk', incoming, transfer, precision=HIGHEST)  15.6 us
    unnamed x48, local copies, waits for them, and re-layouts  13.9 us
  transfers between devices with their start and end apart: 17, of which 13 were waited for; matrix products, arithmetic and copies ran while one was open for 1% of the time, Pallas kernels for 0%

profile of v1, /device:TPU:0, one launch (start us, length us, event | category | flops | bytes accessed | tf_op | source)
XLA Modules:
  0.0 518.5 jit_solution(10789600529413978075)
XLA Ops:
  26.1 119.1 %while.24 = (s32[]{:T(128)}, f32[32,128,64]{1,2,0:T(8,128)S(1)}, f32[4,32,32,128]{3,1,2,0:T(8,128)}, f32[4,32,32,64]{3,2,1,0:T(8,128)S(1)}, f32[4,32,32,64]{3,2,...) while((s32[]{:T(128)}, f32[32,128,64]{1,2,0:T(8,128)S(1)}, ...), condition=%wide.region_3.4_spmd, body=%wide.region_0.3_spmd.sunk | while | flops 809539584 | bytes 26289764 | solution.py:143
  158.3 189.7 %while.25 = (s32[]{:T(128)}, f32[32,64,64]{2,1,0:T(8,128)}, f32[32,64,64]{2,1,0:T(8,128)}, f32[32,64,64]{2,1,0:T(8,128)S(1)}, f32[32,64,64]{2,1,0:T(8,128)S(1)}, /*index=5*/s32[]{:T(128)}) while((s32[]{:T(128)}, f32[32,64,64]{2,1,0:T(8,128)}, f32[32,64,64]{2,1,0:T(8,128)}, f32[32,64,64]{2,1,0:T(8,128)S(1)}, f32[32,64,64]{2,1,0:T(8,128)S(1)}, ...), condition=%wide.region_5.6_spmd, body=%wide.region_4.5_spmd.sunk | while | flops 100794368 | bytes 6291593 | solution.py:167
  163.3 22.7 %collective-permute-done = f32[32,64,64]{2,1,0:T(8,128)S(1)} collective-permute-done((f32[32,64,64]{2,1,0:T(8,128)}, f32[32,64,64]{2,1,0:T(8,128)S(1)}, u32[]{:S(2)}, u32[]{:S(2)}) %collective-permute-start) | collective-permute-done | bytes 524320 | tf_op jit(solution)/shard_map/while/body/eval_jaxpr/ppermute | solution.py:37
  192.5 21.8 %collective-permute-done = f32[32,64,64]{2,1,0:T(8,128)S(1)} collective-permute-done((f32[32,64,64]{2,1,0:T(8,128)}, f32[32,64,64]{2,1,0:T(8,128)S(1)}, u32[]{:S(2)}, u32[]{:S(2)}) %collective-permute-start) | collective-permute-done | bytes 524320 | tf_op jit(solution)/shard_map/while/body/eval_jaxpr/ppermute | solution.py:37
  220.9 20.9 %collective-permute-done = f32[32,64,64]{2,1,0:T(8,128)S(1)} collective-permute-done((f32[32,64,64]{2,1,0:T(8,128)}, f32[32,64,64]{2,1,0:T(8,128)S(1)}, u32[]{:S(2)}, u32[]{:S(2)}) %collective-permute-start) | collective-permute-done | bytes 524320 | tf_op jit(solution)/shard_map/while/body/eval_jaxpr/ppermute | solution.py:37
  244.0 5.2 %collective-permute-start = (f32[32,64,64]{2,1,0:T(8,128)}, f32[32,64,64]{2,1,0:T(8,128)S(1)}, u32[]{:S(2)}, u32[]{:S(2)}) collective-permute-start(f32[32,64,64]{2,1,0:T(8,128)} %get-tuple-element.277), channel_id=1, source_target_pairs={{0,2},{2,4},{4,6},{6,8},{8,10},{10,12},{12,14},{1,3},{3,5},{5,7},{... | collective-permute-start | bytes 1572872 | tf_op jit(solution)/shard_map/while/body/eval_jaxpr/ppermute | solution.py:37
  249.2 19.9 %collective-permute-done = f32[32,64,64]{2,1,0:T(8,128)S(1)} collective-permute-done((f32[32,64,64]{2,1,0:T(8,128)}, f32[32,64,64]{2,1,0:T(8,128)S(1)}, u32[]{:S(2)}, u32[]{:S(2)}) %collective-permute-start) | collective-permute-done | bytes 524320 | tf_op jit(solution)/shard_map/while/body/eval_jaxpr/ppermute | solution.py:37
  271.4 5.2 %collective-permute-start = (f32[32,64,64]{2,1,0:T(8,128)}, f32[32,64,64]{2,1,0:T(8,128)S(1)}, u32[]{:S(2)}, u32[]{:S(2)}) collective-permute-start(f32[32,64,64]{2,1,0:T(8,128)} %get-tuple-element.277), channel_id=1, source_target_pairs={{0,2},{2,4},{4,6},{6,8},{8,10},{10,12},{12,14},{1,3},{3,5},{5,7},{... | collective-permute-start | bytes 1572872 | tf_op jit(solution)/shard_map/while/body/eval_jaxpr/ppermute | solution.py:37
  276.6 19.0 %collective-permute-done = f32[32,64,64]{2,1,0:T(8,128)S(1)} collective-permute-done((f32[32,64,64]{2,1,0:T(8,128)}, f32[32,64,64]{2,1,0:T(8,128)S(1)}, u32[]{:S(2)}, u32[]{:S(2)}) %collective-permute-start) | collective-permute-done | bytes 524320 | tf_op jit(solution)/shard_map/while/body/eval_jaxpr/ppermute | solution.py:37
  297.9 5.2 %collective-permute-start = (f32[32,64,64]{2,1,0:T(8,128)}, f32[32,64,64]{2,1,0:T(8,128)S(1)}, u32[]{:S(2)}, u32[]{:S(2)}) collective-permute-start(f32[32,64,64]{2,1,0:T(8,128)} %get-tuple-element.277), channel_id=1, source_target_pairs={{0,2},{2,4},{4,6},{6,8},{8,10},{10,12},{12,14},{1,3},{3,5},{5,7},{... | collective-permute-start | bytes 1572872 | tf_op jit(solution)/shard_map/while/body/eval_jaxpr/ppermute | solution.py:37
  303.1 18.1 %collective-permute-done = f32[32,64,64]{2,1,0:T(8,128)S(1)} collective-permute-done((f32[32,64,64]{2,1,0:T(8,128)}, f32[32,64,64]{2,1,0:T(8,128)S(1)}, u32[]{:S(2)}, u32[]{:S(2)}) %collective-permute-start) | collective-permute-done | bytes 524320 | tf_op jit(solution)/shard_map/while/body/eval_jaxpr/ppermute | solution.py:37
  323.4 5.2 %collective-permute-start = (f32[32,64,64]{2,1,0:T(8,128)}, f32[32,64,64]{2,1,0:T(8,128)S(1)}, u32[]{:S(2)}, u32[]{:S(2)}) collective-permute-start(f32[32,64,64]{2,1,0:T(8,128)} %get-tuple-element.277), channel_id=1, source_target_pairs={{0,2},{2,4},{4,6},{6,8},{8,10},{10,12},{12,14},{1,3},{3,5},{5,7},{... | collective-permute-start | bytes 1572872 | tf_op jit(solution)/shard_map/while/body/eval_jaxpr/ppermute | solution.py:37
  328.7 17.2 %collective-permute-done = f32[32,64,64]{2,1,0:T(8,128)S(1)} collective-permute-done((f32[32,64,64]{2,1,0:T(8,128)}, f32[32,64,64]{2,1,0:T(8,128)S(1)}, u32[]{:S(2)}, u32[]{:S(2)}) %collective-permute-start) | collective-permute-done | bytes 524320 | tf_op jit(solution)/shard_map/while/body/eval_jaxpr/ppermute | solution.py:37
  348.1 7.0 %fusion.66 = (f32[128,32]{0,1:T(8,128)S(1)}, f32[128,32,64]{0,2,1:T(8,128)S(1)}) fusion(f32[128,32,64]{0,2,1:T(8,128)} %copy.99, f32[32,64,64]{2,1,0:T(8,128)} %get-tuple-element.73, f32[128,32,64]{2,1,0:T(8,128)} %get-tuple-element.146), kind=kOutput, calls=%fused_computation.134 | convolution fusion | flops 201846784 | bytes 3686400 | tf_op jit(solution)/shard_map/hvk,thk->thv/dot_general | solution.py:168
  374.3 6.8 %collective-permute-start.6 = (bf16[1,8,8,2048]{3,2,1,0:T(8,128)(2,1)S(1)}, bf16[1,8,8,2048]{3,2,1,0:T(8,128)(2,1)S(1)}, u32[]{:S(2)}, u32[]{:S(2)}) collective-permute-start(bf16[1,8,8,2048]{3,2,1,0:T(8,128)(2,1)S(1)} %copy.107), channel_id=1, source_target_pairs={{0,12},{2,14},{4,8},{6,10},{8,4},{10,6},{12,0},{14,2},{1,13},{3,15... | collective-permute-start | bytes 786440 | tf_op jit(solution)/shard_map/ppermute | solution.py:26
  385.9 14.0 %collective-permute-done.4 = bf16[1,8,8,2048]{3,2,1,0:T(8,128)(2,1)S(1)} collective-permute-done((bf16[1,8,8,2048]{3,2,1,0:T(8,128)(2,1)S(1)}, bf16[1,8,8,2048]{3,2,1,0:T(8,128)(2,1)S(1)}, u32[]{:S(2)}, u32[]{:S(2)}) %collective-permute-start.4) | collective-permute-done | bytes 262176 | tf_op jit(solution)/shard_map/ppermute | solution.py:26
  399.9 6.0 %collective-permute-done.5 = bf16[1,8,8,2048]{3,2,1,0:T(8,128)(2,1)S(1)} collective-permute-done((bf16[1,8,8,2048]{3,2,1,0:T(8,128)(2,1)S(1)}, bf16[1,8,8,2048]{3,2,1,0:T(8,128)(2,1)S(1)}, u32[]{:S(2)}, u32[]{:S(2)}) %collective-permute-start.5) | collective-permute-done | bytes 262176 | tf_op jit(solution)/shard_map/ppermute | solution.py:26
  406.0 9.1 %convolution_convert_fusion.2 = bf16[512,2048]{1,0:T(8,128)(2,1)} fusion(bf16[512,2048]{1,0:T(8,128)(2,1)S(1)} %bitcast.175, bf16[2048,2048]{1,0:T(8,128)(2,1)} %param.27), kind=kOutput, calls=%fused_computation.68 | convolution fusion | flops 4296015872 | bytes 12582912 | tf_op jit(solution)/shard_map/dot_general | solution.py:223
  416.7 10.8 %all-to-all-start = ((bf16[8,8,16]{2,1,0:T(8,128)(2,1)}), bf16[8,8,16]{2,1,0:T(8,128)(2,1)S(1)}, u32[]{:S(2)}, u32[]{:S(2)}) async-start(bf16[8,8,16]{2,1,0:T(8,128)(2,1)} %bitcast.19), calls=%async_computation | async-start | bytes 32768 | tf_op jit(solution)/shard_map/all_to_all | solution.py:219
  427.7 6.4 %all-to-all-done = bf16[8,8,16]{2,1,0:T(8,128)(2,1)S(1)} async-done(((bf16[8,8,16]{2,1,0:T(8,128)(2,1)}), bf16[8,8,16]{2,1,0:T(8,128)(2,1)S(1)}, u32[]{:S(2)}, u32[]{:S(2)}) %all-to-all-start) | async-done | bytes 2080 | tf_op jit(solution)/shard_map/all_to_all | solution.py:219
  434.1 8.7 %all-reduce.4.cloned.1.call-done = bf16[512,2048]{1,0:T(8,128)(2,1)} async-done(((bf16[512,2048]{1,0:T(8,128)(2,1)}), bf16[512,2048]{1,0:T(8,128)(2,1)}) %all-reduce.4.cloned.1.call-update) | async-done | bytes 2097168 | tf_op jit(solution)/shard_map/psum | solution.py:229
  444.3 9.2 %convolution_convert_fusion.1 = bf16[512,2048]{1,0:T(8,128)(2,1)} fusion(bf16[2048,2048]{1,0:T(8,128)(2,1)} %param.27, f32[512,2048]{1,0:T(8,128)S(1)} %bitcast.173, bf16[512,2048]{1,0:T(8,128)(2,1)S(1)} %copy-done.15, f32[2048]{0:T(1024)S(1)} %copy-done.16, f32[2048]{0:T(1024)S(1)} %broadcast_bitcast_fusion, pred[2048]{0:T(1024)(128)(4,1)S(1)} %fusion.58), kind=kOutput, calls=%fused_computation.67 | convolution fusion | flops 4302307328 | bytes 16795648 | tf_op jit(solution)/shard_map/dot_general | solution.py:233
  453.5 5.8 %all-to-all-start.1 = ((bf16[8,8,8,2048]{3,2,1,0:T(8,128)(2,1)}), bf16[8,8,8,2048]{3,2,1,0:T(8,128)(2,1)S(1)}, u32[]{:S(2)}, u32[]{:S(2)}) async-start(bf16[8,8,8,2048]{3,2,1,0:T(8,128)(2,1)} %bitcast.176), calls=%async_computation.1 | async-start | bytes 4194304 | tf_op jit(solution)/shard_map/all_to_all | solution.py:237
  460.3 47.7 %all-to-all-done.1 = bf16[8,8,8,2048]{3,2,1,0:T(8,128)(2,1)S(1)} async-done(((bf16[8,8,8,2048]{3,2,1,0:T(8,128)(2,1)}), bf16[8,8,8,2048]{3,2,1,0:T(8,128)(2,1)S(1)}, u32[]{:S(2)}, u32[]{:S(2)}) %all-to-all-start.1) | async-done | bytes 2097184 | tf_op jit(solution)/shard_map/all_to_all | solution.py:237
  (260 shorter events, 195.8 us)
Async XLA Ops:
  7.2 420.3 %copy-start = (f32[16]{0:T(128)S(1)}, f32[16]{0:T(128)}, u32[]{:S(2)}) copy-start(f32[16]{0:T(128)} %param.33) | copy-start | bytes 196
  7.2 435.5 %all-reduce.4.cloned.1.call-start = ((), (), s32[]{:S(2)}) async-start(), calls=%async_computation.2 | async-start | bytes 4194304 | tf_op jit(solution)/shard_map/psum | solution.py:229
  13.7 4.2 copy-start.2
  158.3 27.6 %collective-permute-start = (f32[32,64,64]{2,1,0:T(8,128)}, f32[32,64,64]{2,1,0:T(8,128)S(1)}, u32[]{:S(2)}, u32[]{:S(2)}) collective-permute-start(f32[32,64,64]{2,1,0:T(8,128)} %get-tuple-element.277), channel_id=1, source_target_pairs={{0,2},{2,4},{4,6},{6,8},{8,10},{10,12},{12,14},{1,3},{3,5},{5,7},{... | collective-permute-start | bytes 1572872 | tf_op jit(solution)/shard_map/while/body/eval_jaxpr/ppermute | solution.py:37
  188.2 26.1 %collective-permute-start = (f32[32,64,64]{2,1,0:T(8,128)}, f32[32,64,64]{2,1,0:T(8,128)S(1)}, u32[]{:S(2)}, u32[]{:S(2)}) collective-permute-start(f32[32,64,64]{2,1,0:T(8,128)} %get-tuple-element.277), channel_id=1, source_target_pairs={{0,2},{2,4},{4,6},{6,8},{8,10},{10,12},{12,14},{1,3},{3,5},{5,7},{... | collective-permute-start | bytes 1572872 | tf_op jit(solution)/shard_map/while/body/eval_jaxpr/ppermute | solution.py:37
  216.5 25.2 %collective-permute-start = (f32[32,64,64]{2,1,0:T(8,128)}, f32[32,64,64]{2,1,0:T(8,128)S(1)}, u32[]{:S(2)}, u32[]{:S(2)}) collective-permute-start(f32[32,64,64]{2,1,0:T(8,128)} %get-tuple-element.277), channel_id=1, source_target_pairs={{0,2},{2,4},{4,6},{6,8},{8,10},{10,12},{12,14},{1,3},{3,5},{5,7},{... | collective-permute-start | bytes 1572872 | tf_op jit(solution)/shard_map/while/body/eval_jaxpr/ppermute | solution.py:37
  244.0 25.2 %collective-permute-start = (f32[32,64,64]{2,1,0:T(8,128)}, f32[32,64,64]{2,1,0:T(8,128)S(1)}, u32[]{:S(2)}, u32[]{:S(2)}) collective-permute-start(f32[32,64,64]{2,1,0:T(8,128)} %get-tuple-element.277), channel_id=1, source_target_pairs={{0,2},{2,4},{4,6},{6,8},{8,10},{10,12},{12,14},{1,3},{3,5},{5,7},{... | collective-permute-start | bytes 1572872 | tf_op jit(solution)/shard_map/while/body/eval_jaxpr/ppermute | solution.py:37
  271.4 24.2 %collective-permute-start = (f32[32,64,64]{2,1,0:T(8,128)}, f32[32,64,64]{2,1,0:T(8,128)S(1)}, u32[]{:S(2)}, u32[]{:S(2)}) collective-permute-start(f32[32,64,64]{2,1,0:T(8,128)} %get-tuple-element.277), channel_id=1, source_target_pairs={{0,2},{2,4},{4,6},{6,8},{8,10},{10,12},{12,14},{1,3},{3,5},{5,7},{... | collective-permute-start | bytes 1572872 | tf_op jit(solution)/shard_map/while/body/eval_jaxpr/ppermute | solution.py:37
  297.9 23.3 %collective-permute-start = (f32[32,64,64]{2,1,0:T(8,128)}, f32[32,64,64]{2,1,0:T(8,128)S(1)}, u32[]{:S(2)}, u32[]{:S(2)}) collective-permute-start(f32[32,64,64]{2,1,0:T(8,128)} %get-tuple-element.277), channel_id=1, source_target_pairs={{0,2},{2,4},{4,6},{6,8},{8,10},{10,12},{12,14},{1,3},{3,5},{5,7},{... | collective-permute-start | bytes 1572872 | tf_op jit(solution)/shard_map/while/body/eval_jaxpr/ppermute | solution.py:37
  323.4 22.4 %collective-permute-start = (f32[32,64,64]{2,1,0:T(8,128)}, f32[32,64,64]{2,1,0:T(8,128)S(1)}, u32[]{:S(2)}, u32[]{:S(2)}) collective-permute-start(f32[32,64,64]{2,1,0:T(8,128)} %get-tuple-element.277), channel_id=1, source_target_pairs={{0,2},{2,4},{4,6},{6,8},{8,10},{10,12},{12,14},{1,3},{3,5},{5,7},{... | collective-permute-start | bytes 1572872 | tf_op jit(solution)/shard_map/while/body/eval_jaxpr/ppermute | solution.py:37
  355.3 3.9 copy-start.3
  355.3 3.9 copy-start.8
  355.3 3.9 copy-start.10
  363.0 11.3 %collective-permute-start.1 = (bf16[1,8,8,2048]{3,2,1,0:T(8,128)(2,1)S(1)}, bf16[1,8,8,2048]{3,2,1,0:T(8,128)(2,1)S(1)}, u32[]{:S(2)}, u32[]{:S(2)}) collective-permute-start(bf16[1,8,8,2048]{3,2,1,0:T(8,128)(2,1)S(1)} %copy.102), channel_id=1, source_target_pairs={{0,2},{2,0},{4,6},{6,4},{8,10},{10,8},{12,14},{14,12},{1,3},{3,1},... | collective-permute-start | bytes 786440 | tf_op jit(solution)/shard_map/ppermute | solution.py:26
  366.4 14.7 %collective-permute-start.2 = (bf16[1,8,8,2048]{3,2,1,0:T(8,128)(2,1)S(1)}, bf16[1,8,8,2048]{3,2,1,0:T(8,128)(2,1)S(1)}, u32[]{:S(2)}, u32[]{:S(2)}) collective-permute-start(bf16[1,8,8,2048]{3,2,1,0:T(8,128)(2,1)S(1)} %copy.103), channel_id=1, source_target_pairs={{0,4},{2,6},{4,0},{6,2},{8,12},{10,14},{12,8},{14,10},{1,5},{3,7},... | collective-permute-start | bytes 786440 | tf_op jit(solution)/shard_map/ppermute | solution.py:26
  368.5 17.3 %collective-permute-start.3 = (bf16[1,8,8,2048]{3,2,1,0:T(8,128)(2,1)S(1)}, bf16[1,8,8,2048]{3,2,1,0:T(8,128)(2,1)S(1)}, u32[]{:S(2)}, u32[]{:S(2)}) collective-permute-start(bf16[1,8,8,2048]{3,2,1,0:T(8,128)(2,1)S(1)} %copy.104), channel_id=1, source_target_pairs={{0,6},{2,4},{4,2},{6,0},{8,14},{10,12},{12,10},{14,8},{1,7},{3,5},... | collective-permute-start | bytes 786440 | tf_op jit(solution)/shard_map/ppermute | solution.py:26
  370.2 29.7 %collective-permute-start.4 = (bf16[1,8,8,2048]{3,2,1,0:T(8,128)(2,1)S(1)}, bf16[1,8,8,2048]{3,2,1,0:T(8,128)(2,1)S(1)}, u32[]{:S(2)}, u32[]{:S(2)}) collective-permute-start(bf16[1,8,8,2048]{3,2,1,0:T(8,128)(2,1)S(1)} %copy.105), channel_id=1, source_target_pairs={{0,8},{2,10},{4,12},{6,14},{8,0},{10,2},{12,4},{14,6},{1,9},{3,11}... | collective-permute-start | bytes 786440 | tf_op jit(solution)/shard_map/ppermute | solution.py:26
  373.4 32.4 %collective-permute-start.5 = (bf16[1,8,8,2048]{3,2,1,0:T(8,128)(2,1)S(1)}, bf16[1,8,8,2048]{3,2,1,0:T(8,128)(2,1)S(1)}, u32[]{:S(2)}, u32[]{:S(2)}) collective-permute-start(bf16[1,8,8,2048]{3,2,1,0:T(8,128)(2,1)S(1)} %copy.106), channel_id=1, source_target_pairs={{0,10},{2,8},{4,14},{6,12},{8,2},{10,0},{12,6},{14,4},{1,11},{3,9}... | collective-permute-start | bytes 786440 | tf_op jit(solution)/shard_map/ppermute | solution.py:26
  374.3 31.6 %collective-permute-start.6 = (bf16[1,8,8,2048]{3,2,1,0:T(8,128)(2,1)S(1)}, bf16[1,8,8,2048]{3,2,1,0:T(8,128)(2,1)S(1)}, u32[]{:S(2)}, u32[]{:S(2)}) collective-permute-start(bf16[1,8,8,2048]{3,2,1,0:T(8,128)(2,1)S(1)} %copy.107), channel_id=1, source_target_pairs={{0,12},{2,14},{4,8},{6,10},{8,4},{10,6},{12,0},{14,2},{1,13},{3,15... | collective-permute-start | bytes 786440 | tf_op jit(solution)/shard_map/ppermute | solution.py:26
  381.1 24.8 %collective-permute-start.7 = (bf16[1,8,8,2048]{3,2,1,0:T(8,128)(2,1)S(1)}, bf16[1,8,8,2048]{3,2,1,0:T(8,128)(2,1)S(1)}, u32[]{:S(2)}, u32[]{:S(2)}) collective-permute-start(bf16[1,8,8,2048]{3,2,1,0:T(8,128)(2,1)S(1)} %copy.108), channel_id=1, source_target_pairs={{0,14},{2,12},{4,10},{6,8},{8,6},{10,4},{12,2},{14,0},{1,15},{3,13... | collective-permute-start | bytes 786440 | tf_op jit(solution)/shard_map/ppermute | solution.py:26
  415.1 12.5 %copy-start.14 = (s32[16]{0:T(128)S(1)}, s32[16]{0:T(128)}, u32[]{:S(2)}) copy-start(s32[16]{0:T(128)} %param.32) | copy-start | bytes 196
  416.7 17.3 %all-to-all-start = ((bf16[8,8,16]{2,1,0:T(8,128)(2,1)}), bf16[8,8,16]{2,1,0:T(8,128)(2,1)S(1)}, u32[]{:S(2)}, u32[]{:S(2)}) async-start(bf16[8,8,16]{2,1,0:T(8,128)(2,1)} %bitcast.19), calls=%async_computation | async-start | bytes 32768 | tf_op jit(solution)/shard_map/all_to_all | solution.py:219
  427.7 16.2 %copy-start.16 = (f32[2048]{0:T(1024)S(1)}, f32[2048]{0:T(1024)}, u32[]{:S(2)}) copy-start(f32[2048]{0:T(1024)} %param.28) | copy-start | bytes 24580
  453.5 54.5 %all-to-all-start.1 = ((bf16[8,8,8,2048]{3,2,1,0:T(8,128)(2,1)}), bf16[8,8,8,2048]{3,2,1,0:T(8,128)(2,1)S(1)}, u32[]{:S(2)}, u32[]{:S(2)}) async-start(bf16[8,8,8,2048]{3,2,1,0:T(8,128)(2,1)} %bitcast.176), calls=%async_computation.1 | async-start | bytes 4194304 | tf_op jit(solution)/shard_map/all_to_all | solution.py:237
  (16 other events, 32.8 us)
Sparse Core Ops, SparseCore 0:
  415.3 27.4 all-reduce.3
